TPU v7x, 1024 devices: a whole 8x8x8 slice. The times are simulated.
1024 devices in a mesh: row: 32 (over z, x_hi, core), col: 32 (over y, x_lo).
Axes of the slice: x: 8 (x_hi: 2, x_lo: 4; x = x_hi * 4 + x_lo), y: 8, z: 8, core: 2. Of those that a mesh axis runs over, the one named last changes fastest.
Arguments:
- occ_irrep: int32 [128], replicated, may hold values from 0 to 7
- vir_irrep: int32 [1024], replicated, may hold values from 0 to 7
- w_slab: bfloat16 [12288, 131072], P('row', 'col'), may hold values from -0.046875 to 0.046875
- amplitudes: bfloat16 [256, 131072], P('row', 'col'), may hold values from -6 to 6
Outputs:
- cycle_term: float32 [256, 12288], P('col', 'row')
Inputs may be any that keep to these rules, and one draw needn't show every extreme that they name: `occ_irrep`: D2h irrep labels. `vir_irrep`: D2h irrep labels.
All inputs are finite; a program needn't handle non-finite values.
Results may differ from a plain program's by a relative error of at most 0.0003.
Values may be sent and summed in bfloat16 or wider, within the bound.
No kernel may reach another device: no remote copies, remote signals or barrier semaphores. Data moves between devices by JAX's collectives and lax.ppermute only.
A program may use at most 32 MiB of HBM per device.

v0:
```python
import jax
import jax.numpy as jnp
from jax import lax
from jax.sharding import PartitionSpec as P


def labels(index, occ_irrep, vir_irrep):
    nvir = vir_irrep.shape[0]
    occ_part = jnp.take(occ_irrep, index // nvir)
    vir_part = jnp.take(vir_irrep, index % nvir)
    return jnp.bitwise_xor(occ_part, vir_part)


def body(occ_irrep, vir_irrep, w_slab, amplitudes):
    nrows, width = w_slab.shape
    row_start = lax.axis_index("row") * nrows
    col_start = lax.axis_index("col") * width
    row_labels = labels(row_start + jnp.arange(nrows, dtype=jnp.int32), occ_irrep, vir_irrep)
    col_labels = labels(col_start + jnp.arange(width, dtype=jnp.int32), occ_irrep, vir_irrep)
    keep = row_labels[:, None] == col_labels[None, :]
    masked = jnp.where(keep, w_slab, jnp.zeros_like(w_slab))
    dims = (((1,), (1,)), ((), ()))
    gathered = lax.all_gather(amplitudes, "row", axis=0, tiled=True)
    return lax.psum_scatter(
        lax.dot_general(gathered, masked, dims, preferred_element_type=jnp.float32),
        "col",
        scatter_dimension=0,
        tiled=True,
    )


def solution(mesh):
    placed = (P(), P(), P("row", "col"), P("row", "col"))
    return jax.shard_map(
        body, mesh=mesh, in_specs=placed, out_specs=P("col", "row"), check_vma=False
    )
```

profile of v0, /device:TPU:16, one launch (start us, length us, event | category | flops | bytes accessed | tf_op | source)
XLA Modules:
  0.0 432.4 jit_solution(16501538472023561506)
XLA Ops:
  6.5 0.0 copy-start
  6.5 0.0 copy-start.1
  6.5 0.0 all-gather.2.cloned.1.call-start
  6.5 0.7 all-gather.2.cloned.1.call-update
  7.3 0.0 all-reduce.3.cloned.1.call-start
  7.3 0.2 compare_select_fusion.4
  7.5 0.0 copy-done.1
  7.5 24.7 %gather_fusion.2 = s32[4096]{0:T(1024)S(1)} fusion(s32[128]{0:T(128)S(1)} %copy-done.1, s32[4096]{0:T(1024)S(1)} %broadcast_clamp_fusion.1), kind=kCustom, calls=%fused_computation.2 | custom fusion | bytes 49152 | tf_op jit(solution)/shard_map/jit(_take)/gather | solution.py:9
  32.3 2.7 gather_fusion
  35.0 0.0 copy-done
  35.0 0.0 copy-start.2
  35.0 16.7 %gather_fusion.3 = s32[4096]{0:T(1024)S(1)} fusion(s32[1024]{0:T(1024)S(1)} %copy-done, s32[4096]{0:T(1024)S(1)} %broadcast_clamp_fusion), kind=kCustom, calls=%fused_computation.3 | custom fusion | bytes 49152 | tf_op jit(solution)/shard_map/jit(_take)/gather | solution.py:10
  51.7 1.9 gather_fusion.1
  53.7 67.0 %all-gather.2.cloned.1.call-done = bf16[256,4096]{1,0:T(8,128)(2,1)} async-done(((bf16[8,4096]{1,0:T(8,128)(2,1)}), bf16[256,4096]{1,0:T(8,128)(2,1)}) %all-gather.2.cloned.1.call-update) | async-done | bytes 2097168 | tf_op jit(solution)/shard_map/all_gather | solution.py:23
  120.7 0.0 copy-done.2
  120.7 3.4 fusion.4
  124.1 0.0 all-reduce.3.cloned.1.call-update
  124.1 1.3 dynamic-slice
  126.1 297.8 %all-reduce.3.cloned.1.call-done = f32[256,384]{0,1:T(8,128)} async-done(((f32[256,384]{0,1:T(8,128)}), f32[256,384]{0,1:T(8,128)}) %all-reduce.3.cloned.1.call-update) | async-done | bytes 393232
  423.8 1.0 constant_dynamic-slice_fusion
  424.8 0.7 copy.7
  (7 shorter events, 0.1 us)
Async XLA Ops:
  6.5 28.4 %copy-start = (s32[1024]{0:T(1024)S(1)}, s32[1024]{0:T(1024)}, u32[]{:S(2)}) copy-start(s32[1024]{0:T(1024)} %param.5) | copy-start | bytes 12292
  6.5 0.9 copy-start.1
  6.5 114.1 %all-gather.2.cloned.1.call-start = ((), (), s32[]{:S(2)}) async-start(), calls=%async_computation | async-start | bytes 2162688 | tf_op jit(solution)/shard_map/all_gather | solution.py:23
  7.3 416.5 %all-reduce.3.cloned.1.call-start = ((), (), s32[]{:S(2)}) async-start(), calls=%async_computation.1 | async-start | bytes 786432
  35.0 85.7 %copy-start.2 = (bf16[384,4096]{1,0:T(8,128)(2,1)S(1)}, bf16[384,4096]{1,0:T(8,128)(2,1)}, u32[]{:S(2)}) copy-start(bf16[384,4096]{1,0:T(8,128)(2,1)} %param.6) | copy-start | bytes 9437188
Sparse Core Ops, SparseCore 0:
  11.9 108.7 all-gather.1
  124.2 299.5 all-reduce.2
where the time goes:
time: 433 us; the launch traced here: 432 us
  waiting for transfers between devices  366 us (85%)
  local copies, waits for them, and re-layouts  49 us (11%)
  between operations  14.2 us (3%)
    unnamed x3, waiting for transfers between devices  298 us
    all_gather x1, waiting for transfers between devices, body(): gathered = lax.all_gather(amplitudes, 'row', axis=0, tiled=True)  67 us
    gather x2, local copies, waits for them, and re-layouts, labels(): occ_part = jnp.take(occ_irrep, index // nvir)  27.4 us
    gather x2, local copies, waits for them, and re-layouts, labels(): vir_part = jnp.take(vir_irrep, index % nvir)  18.6 us
  transfers between devices with their start and end apart: 2, of which 2 were waited for; matrix products, arithmetic and copies ran while one was open for 11% of the time, Pallas kernels for 0%

commit v1 on v0

v1 whole, which is shorter than its diff:
```python
import jax
import jax.numpy as jnp
from jax import lax
from jax.sharding import PartitionSpec as P


def spans(start, length, occ_irrep, vir_irrep):
    nvir = vir_irrep.shape[0]
    first, offset = start // nvir, start % nvir
    count = -(-length // nvir)
    vir = lax.dynamic_slice_in_dim(jnp.tile(vir_irrep, count + 1), offset, length, 0)
    position = offset + jnp.arange(length, dtype=jnp.int32)
    occ = jnp.zeros((length,), jnp.int32)
    for step in range(count + 1):
        label = lax.dynamic_index_in_dim(occ_irrep, jnp.minimum(first + step, occ_irrep.shape[0] - 1), 0, False)
        occ = jnp.where(position // nvir == step, label, occ)
    return jnp.bitwise_xor(occ, vir)


def body(occ_irrep, vir_irrep, w_slab, amplitudes):
    nrows, width = w_slab.shape
    here, depth = amplitudes.shape[0], amplitudes.shape[1]
    n_row, n_col = lax.axis_size("row"), lax.axis_size("col")
    row_labels = spans(lax.axis_index("row") * nrows, nrows, occ_irrep, vir_irrep)
    col_labels = spans(lax.axis_index("col") * width, width, occ_irrep, vir_irrep)
    keep = row_labels[:, None] == col_labels[None, :]
    masked = jnp.where(keep, w_slab, jnp.zeros_like(w_slab))

    chips = n_row // 2
    groups = [[2 * chip + core for chip in range(chips)] for core in range(2)]
    copies = jnp.broadcast_to(amplitudes[None], (chips, here, depth))
    own = lax.all_to_all(copies, "row", 0, 0, axis_index_groups=groups).reshape(chips * here, depth)
    other = lax.ppermute(own, "row", [(i, i ^ 1) for i in range(n_row)])

    dims = (((1,), (1,)), ((), ()))
    mine = lax.dot_general(own, masked, dims, preferred_element_type=jnp.float32)
    theirs = lax.dot_general(other, masked, dims, preferred_element_type=jnp.float32)
    is_first = lax.axis_index("row") % 2 == 0
    low, high = jnp.where(is_first, mine, theirs), jnp.where(is_first, theirs, mine)
    parts = jnp.stack([low.reshape(chips, here, nrows), high.reshape(chips, here, nrows)], 1)
    sent = lax.all_to_all(parts.reshape(n_col, here, nrows), "col", 0, 0)
    return sent.sum(0)


def solution(mesh):
    placed = (P(), P(), P("row", "col"), P("row", "col"))
    return jax.shard_map(
        body, mesh=mesh, in_specs=placed, out_specs=P("col", "row"), check_vma=False
    )
```

time: 433 us -> 94.6 us (0.22)
  waiting for transfers between devices: 366 us -> 0.01 us
  blocking collectives: 0 us -> 81 us
  local copies, waits for them, and re-layouts: 49 us -> 1.69 us
  between operations: 14.2 us -> 0.26 us
  other arithmetic: 0.26 us -> 5.12 us
    unnamed x3 -> x0, waiting for transfers between devices: 298 us -> none
    all_to_all x0 -> x2, blocking collectives: none -> 81 us  [the longest x1 49.2 us: body(): lax.all_to_all(copies, 'row', 0, 0, axis_index_groups=groups)]
    all_gather x1 -> x0, waiting for transfers between devices: 67 us -> none  [body(): gathered = lax.all_gather(amplitudes, 'row', axis=0, tiled=True)]
    gather x4 -> x0, local copies, waits for them, and re-layouts: 46 us -> none  [the longest x2 27.4 us: labels(): occ_part = jnp.take(occ_irrep, index // nvir)]
    xor x2, other arithmetic: 0.05 us -> 4.46 us  [spans(): return jnp.bitwise_xor(occ, vir)]
  transfers between devices with their start and end apart: 2 -> 1, of which waited for: 2 -> 0; matrix products, arithmetic and copies ran while one was open for 11% -> 9% of each run, Pallas kernels for 0% -> 0%
where the time goes in v1:
time: 94.6 us; the launch traced here: 94.3 us
  blocking collectives  81 us (86%)
  other arithmetic  5.12 us (5%)
  matrix products  4.36 us (5%)
  starting transfers between devices  1.91 us (2%)
  local copies, waits for them, and re-layouts  1.69 us (2%)
    all_to_all x1, blocking collectives, body(): lax.all_to_all(copies, 'row', 0, 0, axis_index_groups=groups)  49.2 us
    all_to_all x1, blocking collectives, body(): sent = lax.all_to_all(parts.reshape(n_col, here, nrows), 'col', 0, 0)  31.7 us
    xor x2, other arithmetic, spans(): return jnp.bitwise_xor(occ, vir)  4.46 us
    dot_general x1, matrix products, body(): lax.dot_general(own, masked, dims, preferred_element_type=jnp.float32)  3.19 us
    ppermute x1, starting transfers between devices, body(): other = lax.ppermute(own, 'row', [(i, i ^ 1) for i in range(n_row)])  1.91 us
  transfers between devices with their start and end apart: 1, of which 0 were waited for; matrix products, arithmetic and copies ran while one was open for 9% of the time, Pallas kernels for 0%

profile of v1, /device:TPU:16, one launch (start us, length us, event | category | flops | bytes accessed | tf_op | source)
XLA Modules:
  0.0 94.3 jit_solution(17836934332229498160)
XLA Ops:
  0.0 0.0 copy-start.1
  0.0 0.0 copy-start
  0.0 1.0 %broadcast_in_dim.42 = bf16[16,8,4096]{2,1,0:T(8,128)(2,1)S(1)} broadcast(bf16[8,4096]{1,0:T(8,128)(2,1)} %param.7), dimensions={1,2} | broadcast | bytes 1114112 | tf_op jit(solution)/shard_map/broadcast_in_dim | solution.py:31
  1.0 49.2 %all_to_all.10 = bf16[16,8,4096]{2,1,0:T(8,128)(2,1)S(1)} all-to-all(bf16[16,8,4096]{2,1,0:T(8,128)(2,1)S(1)} %broadcast_in_dim.42), channel_id=1, replica_groups={{0,64,128,192,256,320,384,448,512,576,640,704,768,832,896,960},{32,96,1..., dimensions={0} | all-to-all | bytes 2097152 | tf_op jit(solution)/shard_map/all_to_all | solution.py:32
  50.2 1.9 %collective-permute-start = (bf16[128,4096]{1,0:T(8,128)(2,1)S(1)}, bf16[128,4096]{1,0:T(8,128)(2,1)S(1)}, u32[]{:S(2)}, u32[]{:S(2)}) collective-permute-start(bf16[128,4096]{1,0:T(8,128)(2,1)S(1)} %bitcast.30), channel_id=1, source_target_pairs={{0,32},{32,0},{64,96},{96,64},{128,160},{160,128},{192,224},{224,1... | collective-permute-start | bytes 3145736 | tf_op jit(solution)/shard_map/ppermute | solution.py:33
  52.2 0.0 copy-done.1
  52.3 0.0 copy-done
  52.3 0.7 fusion.11
  53.0 1.4 %dynamic-slice_xor_fusion.1 = s32[384]{0:T(512)S(1)} fusion(s32[2048]{0:T(1024)S(1)} %bitcast.31, s32[]{:T(128)S(6)} %select_n.119, s32[]{:T(128)} %bitcast.1, s32[]{:T(128)} %bitcast, s32[]{:T(128)S(6)} %select_n.112), kind=kLoop, calls=%fused_computation.23 | loop fusion | flops 8064 | bytes 3088 | tf_op jit(solution)/shard_map/xor | solution.py:17
  54.4 3.0 %dynamic-slice_xor_fusion = s32[4096]{0:T(1024)S(1)} fusion(s32[5120]{0:T(1024)S(1)} %tile.21, s32[]{:T(128)S(6)} %select_n.133, s32[]{:T(128)} %bitcast.6, s32[]{:T(128)} %bitcast.5, s32[]{:T(128)} %bitcast.4, s32[]{:T(128)} %bitcast.3, s32[]{:T(128)} %bitcast.2, s32[]{:T(128)S(6)} %select_n.120), kind=kLoop, calls=%fused_computation.11 | loop fusion | flops 110592 | bytes 32796 | tf_op jit(solution)/shard_map/xor | solution.py:17
  57.5 0.0 copy-start.2
  57.5 3.2 %fusion.1 = f32[384,128]{0,1:T(8,128)S(1)} fusion(bf16[384,4096]{1,0:T(8,128)(2,1)} %param.6, s32[4096]{0:T(1024)S(1)} %dynamic-slice_xor_fusion, s32[384]{0:T(512)S(1)} %dynamic-slice_xor_fusion.1, bf16[16,8,4096]{2,1,0:T(8,128)(2,1)S(1)} %all_to_all.10), kind=kOutput, calls=%fused_computation.2 | convolution fusion | flops 405798912 | bytes 4408832 | tf_op jit(solution)/shard_map/dot_general | solution.py:36
  60.7 0.0 collective-permute-done
  60.7 0.0 copy-done.2
  60.7 1.2 %select_bitcast_fusion.1 = (f32[16,1,8,384]{3,2,1,0:T(8,128)S(1)}, f32[16,1,8,384]{3,2,1,0:T(8,128)S(1)}) fusion(f32[384,128]{0,1:T(8,128)S(1)} %fusion.1, pred[]{:T(512)S(6)} %eq.52, bf16[128,4096]{1,0:T(8,128)(2,1)S(1)} %collective-permute-done, bf16[384,4096]{1,0:T(8,128)(2,1)S(1)} %copy-done.2, s32[4096]{0:T(1024)S(1)} %dynamic-slice_xor_fusion, ...), kind=kOutput, calls=%fused_computation.5 | convolution fusion | flops 405897216 | bytes 4802049 | tf_op jit(solution)/shard_map/dot_general | solution.py:37
  61.9 31.7 %all_to_all.11 = f32[32,8,384]{2,1,0:T(8,128)S(1)} all-to-all(f32[32,8,384]{2,1,0:T(8,128)S(1)} %bitcast.29), channel_id=1, replica_groups=mesh['row'=32,'col'=32] {'col'}, dimensions={0} | all-to-all | bytes 786432 | tf_op jit(solution)/shard_map/all_to_all | solution.py:41
  93.7 0.6 reduce_sum.9
  (5 shorter events, 0.0 us)
Async XLA Ops:
  0.0 52.2 %copy-start.1 = (s32[1024]{0:T(1024)S(1)}, s32[1024]{0:T(1024)}, u32[]{:S(2)}) copy-start(s32[1024]{0:T(1024)} %param.5) | copy-start | bytes 12292
  0.0 52.3 %copy-start = (s32[128]{0:T(128)S(1)}, s32[128]{0:T(128)}, u32[]{:S(2)}) copy-start(s32[128]{0:T(128)} %param.4) | copy-start | bytes 1540
  50.2 10.5 %collective-permute-start = (bf16[128,4096]{1,0:T(8,128)(2,1)S(1)}, bf16[128,4096]{1,0:T(8,128)(2,1)S(1)}, u32[]{:S(2)}, u32[]{:S(2)}) collective-permute-start(bf16[128,4096]{1,0:T(8,128)(2,1)S(1)} %bitcast.30), channel_id=1, source_target_pairs={{0,32},{32,0},{64,96},{96,64},{128,160},{160,128},{192,224},{224,1... | collective-permute-start | bytes 3145736 | tf_op jit(solution)/shard_map/ppermute | solution.py:33
  57.5 3.2 %copy-start.2 = (bf16[384,4096]{1,0:T(8,128)(2,1)S(1)}, bf16[384,4096]{1,0:T(8,128)(2,1)}, u32[]{:S(2)}) copy-start(bf16[384,4096]{1,0:T(8,128)(2,1)} %param.6) | copy-start | bytes 9437188

commit v2 on v0

v2 whole, which is shorter than its diff:
```python
import jax
import jax.numpy as jnp
from jax import lax
from jax.experimental import pallas as pl
from jax.experimental.pallas import tpu as pltpu
from jax.sharding import PartitionSpec as P

BAND = 128


def against(left, w):
    return lax.dot_general(left, w, (((1,), (1,)), ((), ())), preferred_element_type=jnp.float32)


def band_labels(start, band, occ_ref, vir):
    nocc, nvir = occ_ref.shape[0], vir.shape[1]
    row = start + lax.broadcasted_iota(jnp.int32, (band, 1), 0)
    chosen = lax.broadcasted_iota(jnp.int32, (band, nvir), 1) == row % nvir
    vir_part = jnp.sum(jnp.where(chosen, jnp.broadcast_to(vir, (band, nvir)), 0), axis=1, keepdims=True)
    first = start // nvir
    following = occ_ref[jnp.minimum(first + 1, nocc - 1)]
    return vir_part ^ jnp.where(row // nvir == first, occ_ref[first], following)


def mask_kernel(place_ref, occ_ref, vir_ref, *refs):
    *own_refs, w_ref, masked_ref, mine_ref, sems = refs
    nrows, width = masked_ref.shape
    nvir = vir_ref.shape[1]
    vir = vir_ref[...]
    spans = [pl.ds(start, BAND) for start in range(0, nrows, BAND)]
    copies = [pltpu.make_async_copy(w_ref.at[span], masked_ref.at[span], sems.at[i]) for i, span in enumerate(spans)]
    for copy in copies:
        copy.start()
    col_labels = [vir ^ occ_ref[place_ref[1] // nvir + part] for part in range(width // nvir)]
    for i, (span, copy) in enumerate(zip(spans, copies)):
        row_labels = band_labels(place_ref[0] + i * BAND, BAND, occ_ref, vir)
        copy.wait()
        for part, labels in enumerate(col_labels):
            cols = pl.ds(part * nvir, nvir)
            w = masked_ref[span, cols]
            masked_ref[span, cols] = jnp.where(row_labels == labels, w, jnp.zeros_like(w))
        for s, own_ref in enumerate(own_refs):
            product = against(own_ref[...], masked_ref[span, :])
            mine_ref[s, :, :, span] = product.reshape(mine_ref.shape[1], mine_ref.shape[2], BAND)


def mask_and_multiply(occ_irrep, vir_irrep, w_slab, own, here):
    nrows, width = w_slab.shape
    nvir = vir_irrep.shape[0]
    rows = own[0].shape[0]
    place = jnp.stack([lax.axis_index("row") * nrows, lax.axis_index("col") * width]).astype(jnp.int32)
    smem, vmem = pl.BlockSpec(memory_space=pltpu.SMEM), pl.BlockSpec(memory_space=pltpu.VMEM)
    return pl.pallas_call(
        mask_kernel,
        in_specs=[smem, smem, vmem] + [vmem] * len(own) + [pl.BlockSpec(memory_space=pltpu.HBM)],
        out_specs=[vmem, vmem],
        out_shape=[
            jax.ShapeDtypeStruct(w_slab.shape, w_slab.dtype),
            jax.ShapeDtypeStruct((len(own), rows // here, here, nrows), jnp.float32),
        ],
        scratch_shapes=[pltpu.SemaphoreType.DMA((nrows // BAND,))],
        compiler_params=pltpu.CompilerParams(vmem_limit_bytes=48 * 1024 * 1024),
        cost_estimate=pl.CostEstimate(
            flops=2 * len(own) * rows * width * nrows, bytes_accessed=4 * nrows * width, transcendentals=0
        ),
    )(place, occ_irrep, vir_irrep.reshape(1, nvir), *own, w_slab)


def place_kernel(me_ref, other_ref, w_ref, mine_ref, out_ref):
    me = me_ref[0]
    core, side = me % 2, me // 2 % 2
    count, chips, here, nrows = mine_ref.shape
    product = against(other_ref[...], w_ref[...]).reshape(mine_ref.shape)
    for s in range(count):
        if count == 1:
            out_ref[:, pl.ds(core, 1)] = mine_ref[s][:, None]
            out_ref[:, pl.ds(1 - core, 1)] = product[s][:, None]
        else:
            out_ref[:, pl.ds(side ^ s, 1), pl.ds(core, 1)] = mine_ref[s][:, None, None]
            out_ref[:, pl.ds(side ^ s, 1), pl.ds(1 - core, 1)] = product[s][:, None, None]


def multiply_and_place(other, masked, mine):
    nrows, width = masked.shape
    count, chips, here, _ = mine.shape
    shape = (chips, 2, here, nrows) if count == 1 else (chips, count, 2, here, nrows)
    me = lax.axis_index("row").astype(jnp.int32).reshape(1)
    vmem = pl.BlockSpec(memory_space=pltpu.VMEM)
    return pl.pallas_call(
        place_kernel,
        in_specs=[pl.BlockSpec(memory_space=pltpu.SMEM), vmem, vmem, vmem],
        out_specs=vmem,
        out_shape=jax.ShapeDtypeStruct(shape, jnp.float32),
        compiler_params=pltpu.CompilerParams(vmem_limit_bytes=8 * 1024 * 1024),
        cost_estimate=pl.CostEstimate(
            flops=2 * other.shape[0] * width * nrows, bytes_accessed=2 * nrows * width, transcendentals=0
        ),
    )(me, other, masked, mine)


def body(occ_irrep, vir_irrep, w_slab, amplitudes):
    nrows, width = w_slab.shape
    here = amplitudes.shape[0]
    n_row = lax.axis_size("row")
    chips = n_row // 2
    cores = [[2 * chip + core for chip in range(chips)] for core in range(2)]
    copies = jnp.broadcast_to(amplitudes[None], (chips, here, width))
    own = lax.all_to_all(copies, "row", 0, 0, axis_index_groups=cores).reshape(chips * here, width)
    other = lax.ppermute(own, "row", [(i, i ^ 1) for i in range(n_row)])
    masked, mine = mask_and_multiply(occ_irrep, vir_irrep, w_slab, [own], here)
    parts = multiply_and_place(other, masked, mine)
    sent = lax.all_to_all(parts.reshape(n_row, here, nrows), "col", 0, 0)
    return sent.sum(0)


def solution(mesh):
    placed = (P(), P(), P("row", "col"), P("row", "col"))
    return jax.shard_map(
        body, mesh=mesh, in_specs=placed, out_specs=P("col", "row"), check_vma=False
    )
```

time: 433 us -> 89.7 us (0.21)
  waiting for transfers between devices: 366 us -> 0.01 us
  blocking collectives: 0 us -> 81 us
  local copies, waits for them, and re-layouts: 49 us -> 0.97 us
  between operations: 14.2 us -> 0.05 us
  Pallas kernels: 0 us -> 4.82 us
    unnamed x3 -> x0, waiting for transfers between devices: 298 us -> none
    all_to_all x0 -> x2, blocking collectives: none -> 81 us  [the longest x1 49.2 us: body(): lax.all_to_all(copies, 'row', 0, 0, axis_index_groups=cores)]
    all_gather x1 -> x0, waiting for transfers between devices: 67 us -> none  [body(): gathered = lax.all_gather(amplitudes, 'row', axis=0, tiled=True)]
    gather x4 -> x0, local copies, waits for them, and re-layouts: 46 us -> none  [the longest x2 27.4 us: labels(): occ_part = jnp.take(occ_irrep, index // nvir)]
    pallas_call x0 -> x2, Pallas kernels: none -> 4.82 us  [the longest x1 3.74 us: mask_and_multiply(): pl.pallas_call(mask_kernel, in_specs=[smem, smem, vmem] + [vmem] * len(ow...]
  transfers between devices with their start and end apart: 2 -> 1, of which waited for: 2 -> 0; matrix products, arithmetic and copies ran while one was open for 11% -> 0% of each run, Pallas kernels for 0% -> 4%
where the time goes in v2:
time: 89.7 us; the launch traced here: 89.4 us
  blocking collectives  81 us (90%)
  Pallas kernels  4.82 us (5%)
  starting transfers between devices  1.91 us (2%)
  local copies, waits for them, and re-layouts  0.97 us (1%)
    all_to_all x1, blocking collectives, body(): lax.all_to_all(copies, 'row', 0, 0, axis_index_groups=cores)  49.2 us
    all_to_all x1, blocking collectives, body(): sent = lax.all_to_all(parts.reshape(n_row, here, nrows), 'col', 0, 0)  31.8 us
    pallas_call x1, Pallas kernels, mask_and_multiply(): pl.pallas_call(mask_kernel, in_specs=[smem, smem, vmem] + [vmem] * len(ow...  3.74 us
    ppermute x1, starting transfers between devices, body(): other = lax.ppermute(own, 'row', [(i, i ^ 1) for i in range(n_row)])  1.91 us
  transfers between devices with their start and end apart: 1, of which 0 were waited for; matrix products, arithmetic and copies ran while one was open for 0% of the time, Pallas kernels for 4%

profile of v2, /device:TPU:16, one launch (start us, length us, event | category | flops | bytes accessed | tf_op | source)
XLA Modules:
  0.0 89.4 jit_solution(14923006231199836373)
XLA Ops:
  0.0 0.0 copy-start
  0.0 0.0 copy-start.1
  0.0 1.0 %broadcast_in_dim.2 = bf16[16,8,4096]{2,1,0:T(8,128)(2,1)S(1)} broadcast(bf16[8,4096]{1,0:T(8,128)(2,1)} %param.7), dimensions={1,2} | broadcast | bytes 1114112 | tf_op jit(solution)/shard_map/broadcast_in_dim | solution.py:107
  1.0 49.2 %all_to_all.10 = bf16[16,8,4096]{2,1,0:T(8,128)(2,1)S(1)} all-to-all(bf16[16,8,4096]{2,1,0:T(8,128)(2,1)S(1)} %broadcast_in_dim.2), channel_id=1, replica_groups={{0,64,128,192,256,320,384,448,512,576,640,704,768,832,896,960},{32,96,1..., dimensions={0} | all-to-all | bytes 2097152 | tf_op jit(solution)/shard_map/all_to_all | solution.py:108
  50.2 1.9 %collective-permute-start = (bf16[128,4096]{1,0:T(8,128)(2,1)S(1)}, bf16[128,4096]{1,0:T(8,128)(2,1)S(1)}, u32[]{:S(2)}, u32[]{:S(2)}) collective-permute-start(bf16[128,4096]{1,0:T(8,128)(2,1)S(1)} %bitcast.6), channel_id=1, source_target_pairs={{0,32},{32,0},{64,96},{96,64},{128,160},{160,128},{192,224},{224,1... | collective-permute-start | bytes 3145736 | tf_op jit(solution)/shard_map/ppermute | solution.py:109
  52.1 0.1 pad_add_fusion.place_ref
  52.2 0.0 copy-done
  52.2 0.0 copy-done.1
  52.2 3.7 %shard_map.46 = (bf16[384,4096]{1,0:T(8,128)(2,1)S(1)}, f32[1,16,8,384]{3,2,1,0:T(8,128)S(1)}) custom-call(s32[2]{0:T(128)S(1)} %pad_add_fusion.place_ref, s32[128]{0:T(128)S(1)} %copy-done.1, s32[1,1024]{1,0:T(1,128)S(1)} %bitcast.9, bf16[128,4096]{1,0:T(8,128)(2,1)S(1)} %bitcast.7, bf16[384,4096]{1,0:T(8,128)(2,1)} %refs_1_.1), custom_call_target="tpu_custom_call" | custom-call | flops 402653184 | bytes 6291456 | tf_op jit(solution)/shard_map/pallas_call | solution.py:53
  56.0 0.0 collective-permute-done.other_ref
  56.0 1.1 %shard_map.47 = f32[16,2,8,384]{3,2,1,0:T(8,128)S(1)} custom-call(s32[1]{0:T(128)} %bitcast.me_ref, bf16[128,4096]{1,0:T(8,128)(2,1)S(1)} %collective-permute-done.other_ref, bf16[384,4096]{1,0:T(8,128)(2,1)S(1)} %get-tuple-element.7.w_ref, f32[1,16,8,384]{3,2,1,0:T(8,128)S(1)} %get-tuple-element.8.mine_ref), custom_call_target="tpu_custom_call" | custom-call | flops 402653184 | bytes 3145728 | tf_op jit(solution)/shard_map/pallas_call | solution.py:89
  57.1 31.8 %all_to_all.11 = f32[32,8,384]{2,1,0:T(8,128)S(1)} all-to-all(f32[32,8,384]{2,1,0:T(8,128)S(1)} %bitcast.8), channel_id=1, replica_groups=mesh['row'=32,'col'=32] {'col'}, dimensions={0} | all-to-all | bytes 786432 | tf_op jit(solution)/shard_map/all_to_all | solution.py:112
  88.8 0.6 reduce_sum.9
Async XLA Ops:
  0.0 52.2 %copy-start = (s32[1024]{0:T(1024)S(1)}, s32[1024]{0:T(1024)}, u32[]{:S(2)}) copy-start(s32[1024]{0:T(1024)} %param.5) | copy-start | bytes 12292
  0.0 52.2 %copy-start.1 = (s32[128]{0:T(128)S(1)}, s32[128]{0:T(128)}, u32[]{:S(2)}) copy-start(s32[128]{0:T(128)} %occ_ref.1) | copy-start | bytes 1540
  50.2 5.8 %collective-permute-start = (bf16[128,4096]{1,0:T(8,128)(2,1)S(1)}, bf16[128,4096]{1,0:T(8,128)(2,1)S(1)}, u32[]{:S(2)}, u32[]{:S(2)}) collective-permute-start(bf16[128,4096]{1,0:T(8,128)(2,1)S(1)} %bitcast.6), channel_id=1, source_target_pairs={{0,32},{32,0},{64,96},{96,64},{128,160},{160,128},{192,224},{224,1... | collective-permute-start | bytes 3145736 | tf_op jit(solution)/shard_map/ppermute | solution.py:109

commit v3 on v2

--- a/solution.py
+++ b/solution.py
@@ -32,16 +32,25 @@
     for copy in copies:
         copy.start()
     col_labels = [vir ^ occ_ref[place_ref[1] // nvir + part] for part in range(width // nvir)]
-    for i, (span, copy) in enumerate(zip(spans, copies)):
+
+    def mask(i):
         row_labels = band_labels(place_ref[0] + i * BAND, BAND, occ_ref, vir)
-        copy.wait()
+        copies[i].wait()
         for part, labels in enumerate(col_labels):
             cols = pl.ds(part * nvir, nvir)
-            w = masked_ref[span, cols]
-            masked_ref[span, cols] = jnp.where(row_labels == labels, w, jnp.zeros_like(w))
+            w = masked_ref[spans[i], cols]
+            masked_ref[spans[i], cols] = jnp.where(row_labels == labels, w, jnp.zeros_like(w))
+
+    def multiply(i):
         for s, own_ref in enumerate(own_refs):
-            product = against(own_ref[...], masked_ref[span, :])
-            mine_ref[s, :, :, span] = product.reshape(mine_ref.shape[1], mine_ref.shape[2], BAND)
+            product = against(own_ref[...], masked_ref[spans[i], :])
+            mine_ref[s, :, :, spans[i]] = product.reshape(mine_ref.shape[1], mine_ref.shape[2], BAND)
+
+    for i in range(len(spans)):
+        mask(i)
+        if i:
+            multiply(i - 1)
+    multiply(len(spans) - 1)
 
 
 def mask_and_multiply(occ_irrep, vir_irrep, w_slab, own, here):
@@ -67,23 +76,19 @@
 
 
 def place_kernel(me_ref, other_ref, w_ref, mine_ref, out_ref):
-    me = me_ref[0]
-    core, side = me % 2, me // 2 % 2
-    count, chips, here, nrows = mine_ref.shape
+    core = me_ref[0] % 2
+    planes = out_ref.shape[0]
     product = against(other_ref[...], w_ref[...]).reshape(mine_ref.shape)
-    for s in range(count):
-        if count == 1:
-            out_ref[:, pl.ds(core, 1)] = mine_ref[s][:, None]
-            out_ref[:, pl.ds(1 - core, 1)] = product[s][:, None]
-        else:
-            out_ref[:, pl.ds(side ^ s, 1), pl.ds(core, 1)] = mine_ref[s][:, None, None]
-            out_ref[:, pl.ds(side ^ s, 1), pl.ds(1 - core, 1)] = product[s][:, None, None]
+    for value, at in ((mine_ref, core), (product, 1 - core)):
+        for side in range(2):
+            blocks = value[0, side * planes : (side + 1) * planes]
+            out_ref[:, side, pl.ds(at, 1)] = blocks[:, None]
 
 
 def multiply_and_place(other, masked, mine):
     nrows, width = masked.shape
-    count, chips, here, _ = mine.shape
-    shape = (chips, 2, here, nrows) if count == 1 else (chips, count, 2, here, nrows)
+    _, chips, here, _ = mine.shape
+    shape = (chips // 2, 2, 2, here, nrows)
     me = lax.axis_index("row").astype(jnp.int32).reshape(1)
     vmem = pl.BlockSpec(memory_space=pltpu.VMEM)
     return pl.pallas_call(
@@ -103,7 +108,7 @@
     here = amplitudes.shape[0]
     n_row = lax.axis_size("row")
     chips = n_row // 2
-    cores = [[2 * chip + core for chip in range(chips)] for core in range(2)]
+    cores = [[4 * p + 2 * side + core for side in range(2) for p in range(chips // 2)] for core in range(2)]
     copies = jnp.broadcast_to(amplitudes[None], (chips, here, width))
     own = lax.all_to_all(copies, "row", 0, 0, axis_index_groups=cores).reshape(chips * here, width)
     other = lax.ppermute(own, "row", [(i, i ^ 1) for i in range(n_row)])

time: 89.7 us -> 85.9 us (0.958)
  blocking collectives: 81 us -> 77.5 us
    all_to_all x1, blocking collectives: 31.8 us -> 28.9 us  [body(): sent = lax.all_to_all(parts.reshape(n_row, here, nrows), 'col', 0, 0)]
where the time goes in v3:
time: 85.9 us; the launch traced here: 85.7 us
  blocking collectives  77.5 us (90%)
  Pallas kernels  4.56 us (5%)
  starting transfers between devices  1.91 us (2%)
  local copies, waits for them, and re-layouts  0.97 us (1%)
    all_to_all x1, blocking collectives, body(): lax.all_to_all(copies, 'row', 0, 0, axis_index_groups=cores)  48.6 us
    all_to_all x1, blocking collectives, body(): sent = lax.all_to_all(parts.reshape(n_row, here, nrows), 'col', 0, 0)  28.9 us
    pallas_call x1, Pallas kernels, mask_and_multiply(): pl.pallas_call(mask_kernel, in_specs=[smem, smem, vmem] + [vmem] * len(ow...  3.47 us
    ppermute x1, starting transfers between devices, body(): other = lax.ppermute(own, 'row', [(i, i ^ 1) for i in range(n_row)])  1.91 us
  transfers between devices with their start and end apart: 1, of which 0 were waited for; matrix products, arithmetic and copies ran while one was open for 0% of the time, Pallas kernels for 4%

profile of v3, /device:TPU:16, one launch (start us, length us, event | category | flops | bytes accessed | tf_op | source)
XLA Modules:
  0.0 85.7 jit_solution(7047268939615339002)
XLA Ops:
  0.0 0.0 copy-start
  0.0 0.0 copy-start.1
  0.0 1.0 %broadcast_in_dim.2 = bf16[16,8,4096]{2,1,0:T(8,128)(2,1)S(1)} broadcast(bf16[8,4096]{1,0:T(8,128)(2,1)} %param.7), dimensions={1,2} | broadcast | bytes 1114112 | tf_op jit(solution)/shard_map/broadcast_in_dim | solution.py:112
  1.0 48.6 %all_to_all.10 = bf16[16,8,4096]{2,1,0:T(8,128)(2,1)S(1)} all-to-all(bf16[16,8,4096]{2,1,0:T(8,128)(2,1)S(1)} %broadcast_in_dim.2), channel_id=1, replica_groups={{0,128,256,384,512,640,768,896,64,192,320,448,576,704,832,960},{32,160,..., dimensions={0} | all-to-all | bytes 2097152 | tf_op jit(solution)/shard_map/all_to_all | solution.py:113
  49.6 1.9 %collective-permute-start = (bf16[128,4096]{1,0:T(8,128)(2,1)S(1)}, bf16[128,4096]{1,0:T(8,128)(2,1)S(1)}, u32[]{:S(2)}, u32[]{:S(2)}) collective-permute-start(bf16[128,4096]{1,0:T(8,128)(2,1)S(1)} %bitcast.6), channel_id=1, source_target_pairs={{0,32},{32,0},{64,96},{96,64},{128,160},{160,128},{192,224},{224,1... | collective-permute-start | bytes 3145736 | tf_op jit(solution)/shard_map/ppermute | solution.py:114
  51.5 0.1 pad_add_fusion.place_ref
  51.6 0.0 copy-done
  51.6 0.0 copy-done.1
  51.6 3.5 %shard_map.46 = (bf16[384,4096]{1,0:T(8,128)(2,1)S(1)}, f32[1,16,8,384]{3,2,1,0:T(8,128)S(1)}) custom-call(s32[2]{0:T(128)S(1)} %pad_add_fusion.place_ref, s32[128]{0:T(128)S(1)} %copy-done.1, s32[1,1024]{1,0:T(1,128)S(1)} %bitcast.9, bf16[128,4096]{1,0:T(8,128)(2,1)S(1)} %bitcast.7, bf16[384,4096]{1,0:T(8,128)(2,1)} %refs_1_.1), custom_call_target="tpu_custom_call" | custom-call | flops 402653184 | bytes 6291456 | tf_op jit(solution)/shard_map/pallas_call | solution.py:62
  55.0 0.0 collective-permute-done.other_ref
  55.1 1.1 %shard_map.47 = f32[8,2,2,8,384]{4,3,2,1,0:T(8,128)S(1)} custom-call(s32[1]{0:T(128)} %bitcast.me_ref, bf16[128,4096]{1,0:T(8,128)(2,1)S(1)} %collective-permute-done.other_ref, bf16[384,4096]{1,0:T(8,128)(2,1)S(1)} %get-tuple-element.7.w_ref, f32[1,16,8,384]{3,2,1,0:T(8,128)S(1)} %get-tuple-element.8.mine_ref), custom_call_target="tpu_custom_call" | custom-call | flops 402653184 | bytes 3145728 | tf_op jit(solution)/shard_map/pallas_call | solution.py:94
  56.1 28.9 %all_to_all.11 = f32[32,8,384]{2,1,0:T(8,128)S(1)} all-to-all(f32[32,8,384]{2,1,0:T(8,128)S(1)} %bitcast.8), channel_id=1, replica_groups=mesh['row'=32,'col'=32] {'col'}, dimensions={0} | all-to-all | bytes 786432 | tf_op jit(solution)/shard_map/all_to_all | solution.py:117
  85.0 0.6 reduce_sum.9
Async XLA Ops:
  0.0 51.6 %copy-start = (s32[1024]{0:T(1024)S(1)}, s32[1024]{0:T(1024)}, u32[]{:S(2)}) copy-start(s32[1024]{0:T(1024)} %param.5) | copy-start | bytes 12292
  0.0 51.6 %copy-start.1 = (s32[128]{0:T(128)S(1)}, s32[128]{0:T(128)}, u32[]{:S(2)}) copy-start(s32[128]{0:T(128)} %occ_ref.1) | copy-start | bytes 1540
  49.6 5.5 %collective-permute-start = (bf16[128,4096]{1,0:T(8,128)(2,1)S(1)}, bf16[128,4096]{1,0:T(8,128)(2,1)S(1)}, u32[]{:S(2)}, u32[]{:S(2)}) collective-permute-start(bf16[128,4096]{1,0:T(8,128)(2,1)S(1)} %bitcast.6), channel_id=1, source_target_pairs={{0,32},{32,0},{64,96},{96,64},{128,160},{160,128},{192,224},{224,1... | collective-permute-start | bytes 3145736 | tf_op jit(solution)/shard_map/ppermute | solution.py:114

commit v4 on v3

--- a/solution.py
+++ b/solution.py
@@ -81,8 +81,9 @@
     product = against(other_ref[...], w_ref[...]).reshape(mine_ref.shape)
     for value, at in ((mine_ref, core), (product, 1 - core)):
         for side in range(2):
-            blocks = value[0, side * planes : (side + 1) * planes]
-            out_ref[:, side, pl.ds(at, 1)] = blocks[:, None]
+            for p in range(planes):
+                plane = p + at * (planes - 1 - 2 * p)
+                out_ref[pl.ds(plane, 1), pl.ds(side ^ at, 1), pl.ds(at, 1)] = value[0, side * planes + p][None, None, None]
 
 
 def multiply_and_place(other, masked, mine):
@@ -108,7 +109,9 @@
     here = amplitudes.shape[0]
     n_row = lax.axis_size("row")
     chips = n_row // 2
-    cores = [[4 * p + 2 * side + core for side in range(2) for p in range(chips // 2)] for core in range(2)]
+    planes = chips // 2
+    ways = [(0, 1, range(planes)), (1, 0, range(planes - 1, -1, -1))]
+    cores = [[4 * p + 2 * side + core for side in ways[core][:2] for p in ways[core][2]] for core in range(2)]
     copies = jnp.broadcast_to(amplitudes[None], (chips, here, width))
     own = lax.all_to_all(copies, "row", 0, 0, axis_index_groups=cores).reshape(chips * here, width)
     other = lax.ppermute(own, "row", [(i, i ^ 1) for i in range(n_row)])

time: 85.9 us -> 82.6 us (0.962)
  the two profiles are of different devices: /device:TPU:16 before, /device:TPU:14 now
where the time goes in v4:
time: 82.6 us; the launch traced here: 82.4 us
  blocking collectives  74.2 us (90%)
  Pallas kernels  4.56 us (6%)
  starting transfers between devices  1.91 us (2%)
  local copies, waits for them, and re-layouts  0.97 us (1%)
    all_to_all x1, blocking collectives, body(): lax.all_to_all(copies, 'row', 0, 0, axis_index_groups=cores)  45.3 us
    all_to_all x1, blocking collectives, body(): sent = lax.all_to_all(parts.reshape(n_row, here, nrows), 'col', 0, 0)  28.8 us
    pallas_call x1, Pallas kernels, mask_and_multiply(): pl.pallas_call(mask_kernel, in_specs=[smem, smem, vmem] + [vmem] * len(ow...  3.47 us
    ppermute x1, starting transfers between devices, body(): other = lax.ppermute(own, 'row', [(i, i ^ 1) for i in range(n_row)])  1.91 us
  transfers between devices with their start and end apart: 1, of which 0 were waited for; matrix products, arithmetic and copies ran while one was open for 0% of the time, Pallas kernels for 4%

profile of v4, /device:TPU:14, one launch (start us, length us, event | category | flops | bytes accessed | tf_op | source)
XLA Modules:
  0.0 82.4 jit_solution(13988162565215300597)
XLA Ops:
  0.0 0.0 copy-start
  0.0 0.0 copy-start.1
  0.0 1.0 %broadcast_in_dim.2 = bf16[16,8,4096]{2,1,0:T(8,128)(2,1)S(1)} broadcast(bf16[8,4096]{1,0:T(8,128)(2,1)} %param.7), dimensions={1,2} | broadcast | bytes 1114112 | tf_op jit(solution)/shard_map/broadcast_in_dim | solution.py:115
  1.0 45.3 %all_to_all.10 = bf16[16,8,4096]{2,1,0:T(8,128)(2,1)S(1)} all-to-all(bf16[16,8,4096]{2,1,0:T(8,128)(2,1)S(1)} %broadcast_in_dim.2), channel_id=1, replica_groups={{0,128,256,384,512,640,768,896,64,192,320,448,576,704,832,960},{992,864..., dimensions={0} | all-to-all | bytes 2097152 | tf_op jit(solution)/shard_map/all_to_all | solution.py:116
  46.3 1.9 %collective-permute-start = (bf16[128,4096]{1,0:T(8,128)(2,1)S(1)}, bf16[128,4096]{1,0:T(8,128)(2,1)S(1)}, u32[]{:S(2)}, u32[]{:S(2)}) collective-permute-start(bf16[128,4096]{1,0:T(8,128)(2,1)S(1)} %bitcast.6), channel_id=1, source_target_pairs={{0,32},{32,0},{64,96},{96,64},{128,160},{160,128},{192,224},{224,1... | collective-permute-start | bytes 3145736 | tf_op jit(solution)/shard_map/ppermute | solution.py:117
  48.2 0.1 pad_add_fusion.place_ref
  48.3 0.0 copy-done
  48.3 0.0 copy-done.1
  48.3 3.5 %shard_map.46 = (bf16[384,4096]{1,0:T(8,128)(2,1)S(1)}, f32[1,16,8,384]{3,2,1,0:T(8,128)S(1)}) custom-call(s32[2]{0:T(128)S(1)} %pad_add_fusion.place_ref, s32[128]{0:T(128)S(1)} %copy-done.1, s32[1,1024]{1,0:T(1,128)S(1)} %bitcast.9, bf16[128,4096]{1,0:T(8,128)(2,1)S(1)} %bitcast.7, bf16[384,4096]{1,0:T(8,128)(2,1)} %refs_1_.1), custom_call_target="tpu_custom_call" | custom-call | flops 402653184 | bytes 6291456 | tf_op jit(solution)/shard_map/pallas_call | solution.py:62
  51.8 0.0 collective-permute-done.other_ref
  51.8 1.1 %shard_map.47 = f32[8,2,2,8,384]{4,3,2,1,0:T(8,128)S(1)} custom-call(s32[1]{0:T(128)} %bitcast.me_ref, bf16[128,4096]{1,0:T(8,128)(2,1)S(1)} %collective-permute-done.other_ref, bf16[384,4096]{1,0:T(8,128)(2,1)S(1)} %get-tuple-element.7.w_ref, f32[1,16,8,384]{3,2,1,0:T(8,128)S(1)} %get-tuple-element.8.mine_ref), custom_call_target="tpu_custom_call" | custom-call | flops 402653184 | bytes 3145728 | tf_op jit(solution)/shard_map/pallas_call | solution.py:95
  52.9 28.8 %all_to_all.11 = f32[32,8,384]{2,1,0:T(8,128)S(1)} all-to-all(f32[32,8,384]{2,1,0:T(8,128)S(1)} %bitcast.8), channel_id=1, replica_groups=mesh['row'=32,'col'=32] {'col'}, dimensions={0} | all-to-all | bytes 786432 | tf_op jit(solution)/shard_map/all_to_all | solution.py:120
  81.7 0.6 reduce_sum.9
Async XLA Ops:
  0.0 48.3 %copy-start = (s32[1024]{0:T(1024)S(1)}, s32[1024]{0:T(1024)}, u32[]{:S(2)}) copy-start(s32[1024]{0:T(1024)} %param.5) | copy-start | bytes 12292
  0.0 48.3 %copy-start.1 = (s32[128]{0:T(128)S(1)}, s32[128]{0:T(128)}, u32[]{:S(2)}) copy-start(s32[128]{0:T(128)} %occ_ref.1) | copy-start | bytes 1540
  46.3 5.5 %collective-permute-start = (bf16[128,4096]{1,0:T(8,128)(2,1)S(1)}, bf16[128,4096]{1,0:T(8,128)(2,1)S(1)}, u32[]{:S(2)}, u32[]{:S(2)}) collective-permute-start(bf16[128,4096]{1,0:T(8,128)(2,1)S(1)} %bitcast.6), channel_id=1, source_target_pairs={{0,32},{32,0},{64,96},{96,64},{128,160},{160,128},{192,224},{224,1... | collective-permute-start | bytes 3145736 | tf_op jit(solution)/shard_map/ppermute | solution.py:117

commit v5 on v4

--- a/solution.py
+++ b/solution.py
@@ -28,15 +28,18 @@
     nvir = vir_ref.shape[1]
     vir = vir_ref[...]
     spans = [pl.ds(start, BAND) for start in range(0, nrows, BAND)]
-    copies = [pltpu.make_async_copy(w_ref.at[span], masked_ref.at[span], sems.at[i]) for i, span in enumerate(spans)]
-    for copy in copies:
-        copy.start()
+    areas = [(i, part) for i in range(len(spans)) for part in range(width // nvir)]
+    copies = {}
+    for i, part in areas:
+        area = (spans[i], pl.ds(part * nvir, nvir))
+        copies[i, part] = pltpu.make_async_copy(w_ref.at[area], masked_ref.at[area], sems.at[i, part])
+        copies[i, part].start()
     col_labels = [vir ^ occ_ref[place_ref[1] // nvir + part] for part in range(width // nvir)]
 
     def mask(i):
         row_labels = band_labels(place_ref[0] + i * BAND, BAND, occ_ref, vir)
-        copies[i].wait()
         for part, labels in enumerate(col_labels):
+            copies[i, part].wait()
             cols = pl.ds(part * nvir, nvir)
             w = masked_ref[spans[i], cols]
             masked_ref[spans[i], cols] = jnp.where(row_labels == labels, w, jnp.zeros_like(w))
@@ -67,7 +70,7 @@
             jax.ShapeDtypeStruct(w_slab.shape, w_slab.dtype),
             jax.ShapeDtypeStruct((len(own), rows // here, here, nrows), jnp.float32),
         ],
-        scratch_shapes=[pltpu.SemaphoreType.DMA((nrows // BAND,))],
+        scratch_shapes=[pltpu.SemaphoreType.DMA((nrows // BAND, width // nvir))],
         compiler_params=pltpu.CompilerParams(vmem_limit_bytes=48 * 1024 * 1024),
         cost_estimate=pl.CostEstimate(
             flops=2 * len(own) * rows * width * nrows, bytes_accessed=4 * nrows * width, transcendentals=0

time: 82.6 us -> 82.7 us (level)
  no operation moved by 1% of the time
where the time goes in v5:
time: 82.7 us; the launch traced here: 82.4 us
  blocking collectives  74.2 us (90%)
  Pallas kernels  4.64 us (6%)
  starting transfers between devices  1.91 us (2%)
  local copies, waits for them, and re-layouts  0.97 us (1%)
    all_to_all x1, blocking collectives, body(): lax.all_to_all(copies, 'row', 0, 0, axis_index_groups=cores)  45.3 us
    all_to_all x1, blocking collectives, body(): sent = lax.all_to_all(parts.reshape(n_row, here, nrows), 'col', 0, 0)  28.8 us
    pallas_call x1, Pallas kernels, mask_and_multiply(): pl.pallas_call(mask_kernel, in_specs=[smem, smem, vmem] + [vmem] * len(ow...  3.55 us
    ppermute x1, starting transfers between devices, body(): other = lax.ppermute(own, 'row', [(i, i ^ 1) for i in range(n_row)])  1.91 us
  transfers between devices with their start and end apart: 1, of which 0 were waited for; matrix products, arithmetic and copies ran while one was open for 0% of the time, Pallas kernels for 4%

profile of v5, /device:TPU:14, one launch (start us, length us, event | category | flops | bytes accessed | tf_op | source)
XLA Modules:
  0.0 82.4 jit_solution(5195167573859520352)
XLA Ops:
  0.0 0.0 copy-start
  0.0 0.0 copy-start.1
  0.0 1.0 %broadcast_in_dim.2 = bf16[16,8,4096]{2,1,0:T(8,128)(2,1)S(1)} broadcast(bf16[8,4096]{1,0:T(8,128)(2,1)} %param.7), dimensions={1,2} | broadcast | bytes 1114112 | tf_op jit(solution)/shard_map/broadcast_in_dim | solution.py:118
  1.0 45.3 %all_to_all.10 = bf16[16,8,4096]{2,1,0:T(8,128)(2,1)S(1)} all-to-all(bf16[16,8,4096]{2,1,0:T(8,128)(2,1)S(1)} %broadcast_in_dim.2), channel_id=1, replica_groups={{0,128,256,384,512,640,768,896,64,192,320,448,576,704,832,960},{992,864..., dimensions={0} | all-to-all | bytes 2097152 | tf_op jit(solution)/shard_map/all_to_all | solution.py:119
  46.3 1.9 %collective-permute-start = (bf16[128,4096]{1,0:T(8,128)(2,1)S(1)}, bf16[128,4096]{1,0:T(8,128)(2,1)S(1)}, u32[]{:S(2)}, u32[]{:S(2)}) collective-permute-start(bf16[128,4096]{1,0:T(8,128)(2,1)S(1)} %bitcast.6), channel_id=1, source_target_pairs={{0,32},{32,0},{64,96},{96,64},{128,160},{160,128},{192,224},{224,1... | collective-permute-start | bytes 3145736 | tf_op jit(solution)/shard_map/ppermute | solution.py:120
  48.2 0.1 pad_add_fusion.place_ref
  48.3 0.0 copy-done
  48.3 0.0 copy-done.1
  48.3 3.5 %shard_map.46 = (bf16[384,4096]{1,0:T(8,128)(2,1)S(1)}, f32[1,16,8,384]{3,2,1,0:T(8,128)S(1)}) custom-call(s32[2]{0:T(128)S(1)} %pad_add_fusion.place_ref, s32[128]{0:T(128)S(1)} %copy-done.1, s32[1,1024]{1,0:T(1,128)S(1)} %bitcast.9, bf16[128,4096]{1,0:T(8,128)(2,1)S(1)} %bitcast.7, bf16[384,4096]{1,0:T(8,128)(2,1)} %refs_1_.1), custom_call_target="tpu_custom_call" | custom-call | flops 402653184 | bytes 6291456 | tf_op jit(solution)/shard_map/pallas_call | solution.py:65
  51.9 0.0 collective-permute-done.other_ref
  51.9 1.1 %shard_map.47 = f32[8,2,2,8,384]{4,3,2,1,0:T(8,128)S(1)} custom-call(s32[1]{0:T(128)} %bitcast.me_ref, bf16[128,4096]{1,0:T(8,128)(2,1)S(1)} %collective-permute-done.other_ref, bf16[384,4096]{1,0:T(8,128)(2,1)S(1)} %get-tuple-element.7.w_ref, f32[1,16,8,384]{3,2,1,0:T(8,128)S(1)} %get-tuple-element.8.mine_ref), custom_call_target="tpu_custom_call" | custom-call | flops 402653184 | bytes 3145728 | tf_op jit(solution)/shard_map/pallas_call | solution.py:98
  53.0 28.8 %all_to_all.11 = f32[32,8,384]{2,1,0:T(8,128)S(1)} all-to-all(f32[32,8,384]{2,1,0:T(8,128)S(1)} %bitcast.8), channel_id=1, replica_groups=mesh['row'=32,'col'=32] {'col'}, dimensions={0} | all-to-all | bytes 786432 | tf_op jit(solution)/shard_map/all_to_all | solution.py:123
  81.8 0.6 reduce_sum.9
Async XLA Ops:
  0.0 48.3 %copy-start = (s32[1024]{0:T(1024)S(1)}, s32[1024]{0:T(1024)}, u32[]{:S(2)}) copy-start(s32[1024]{0:T(1024)} %param.5) | copy-start | bytes 12292
  0.0 48.3 %copy-start.1 = (s32[128]{0:T(128)S(1)}, s32[128]{0:T(128)}, u32[]{:S(2)}) copy-start(s32[128]{0:T(128)} %occ_ref.1) | copy-start | bytes 1540
  46.3 5.6 %collective-permute-start = (bf16[128,4096]{1,0:T(8,128)(2,1)S(1)}, bf16[128,4096]{1,0:T(8,128)(2,1)S(1)}, u32[]{:S(2)}, u32[]{:S(2)}) collective-permute-start(bf16[128,4096]{1,0:T(8,128)(2,1)S(1)} %bitcast.6), channel_id=1, source_target_pairs={{0,32},{32,0},{64,96},{96,64},{128,160},{160,128},{192,224},{224,1... | collective-permute-start | bytes 3145736 | tf_op jit(solution)/shard_map/ppermute | solution.py:120
